TPU v7x, 256 devices: a whole 4x4x8 slice. The times are simulated.
256 devices in a mesh: row: 16 (over z, core), col: 16 (over y, x).
Axes of the slice: x: 4, y: 4, z: 8, core: 2. Of those that a mesh axis runs over, the one named last changes fastest.
Arguments:
- src_emb: float32 [32, 262144], P(None, ('row', 'col')), may hold values from -6 to 6
- tgt_emb: float32 [32, 32768], P(None, 'col'), may hold values from -6 to 6
- log_a: float32 [262144], P(('row', 'col')), may hold values from -5 to 5
- log_b: float32 [32768], P('col'), may hold values from -5 to 5
- g_init: float32 [32768], P('col'), may hold values from -15 to 425
- lists: int32 [1024, 16, 4], P('row', 'col'), may hold values from 0 to 7, as said below
- counts: int32 [1024, 16], P('row', 'col'), may hold values from 1 to 4, as said below
Outputs:
- f_pot: float32 [262144], P(('row', 'col'))
- g_pot: float32 [32768], P('col')
Inputs may be any that keep to these rules, and one draw needn't show every extreme that they name: `lists`: within one list the slots hold different blocks, and slot 0 of source block b holds b mod 8. `counts`: source block 0 has all 4 slots valid in every index of col.
All inputs are finite; a program needn't handle non-finite values.
Results may differ from a plain program's by a relative error of at most 0.000067.
Values sent between devices are 32-bit elements; how exact they have to be, the bound alone decides.
A program may use at most 64 MiB of HBM per device.

v0:
```python
import jax
import jax.numpy as jnp
from jax import lax
from jax.sharding import PartitionSpec as P

BLOCK_CELLS = 256


EPSILON = 2.0
NEG = -1e30
GROUP_WIDTH = 4


def combined_all(value, axis, join):
    pieces = jax.tree.map(lambda part: lax.all_gather(part, axis), value)
    head = jax.tree.map(lambda part: part[0], pieces)
    tail = jax.tree.map(lambda part: part[1:], pieces)
    subtotal, _ = lax.scan(lambda subtotal, piece: (join(subtotal, piece), None), head, tail)
    return subtotal


def pair_cost(xb, yb):
    cross = jnp.einsum("gli,gelj->geij", xb, yb, precision=lax.Precision.HIGHEST)
    xx = jnp.sum(xb * xb, axis=1)
    yy = jnp.sum(yb * yb, axis=2)
    return 0.5 * (xx[:, None, :, None] + yy[:, :, None, :]) - cross


def combine(first, second):
    peak_value = jnp.maximum(first[0], second[0])
    return (
        peak_value,
        first[1] * jnp.exp(first[0] - peak_value) + second[1] * jnp.exp(second[0] - peak_value),
    )


def per_device(src_emb, tgt_emb, log_a, log_b, g_init, lists, counts):
    latent_vector = src_emb.shape[0]
    tbc = tgt_emb.shape[1] // BLOCK_CELLS
    cross_dense, weights = (
        lax.all_gather(src_emb, "col", axis=1, tiled=True),
        lax.all_gather(log_a, "col", axis=0, tiled=True),
    )
    sparse_block_rows = cross_dense.shape[1] // BLOCK_CELLS
    slot_table = lists.shape[2]
    group_rows = sparse_block_rows // GROUP_WIDTH
    cross_blocks = (
        cross_dense.reshape(latent_vector, sparse_block_rows, BLOCK_CELLS)
        .transpose(1, 0, 2)
        .reshape(group_rows, GROUP_WIDTH, latent_vector, BLOCK_CELLS)
    )
    yblocks = tgt_emb.reshape(latent_vector, tbc, BLOCK_CELLS).transpose(1, 0, 2)
    gblocks = g_init.reshape(tbc, BLOCK_CELLS)
    cell_index = lists.reshape(sparse_block_rows, slot_table)
    valid = jnp.arange(slot_table, dtype=jnp.int32)[None, :] < counts
    ids_grouped = cell_index.reshape(group_rows, GROUP_WIDTH, slot_table)
    valid_grouped = valid.reshape(group_rows, GROUP_WIDTH, slot_table)

    def row_stats(args):
        xb, chosen, okay = args
        cost = pair_cost(xb, yblocks[chosen])
        score = (gblocks[chosen][:, :, None, :] - cost) / EPSILON
        score = jnp.where(okay[:, :, None, None], score, NEG)
        top = jnp.max(score, axis=(1, 3))
        total = jnp.sum(jnp.exp(score - top[:, None, :, None]), axis=(1, 3))
        return (top, total)

    top, total = lax.map(row_stats, (cross_blocks, ids_grouped, valid_grouped))
    top = top.reshape(-1)
    total = total.reshape(-1)
    top, total = combined_all((top, total), "col", combine)
    f_full = EPSILON * weights - EPSILON * (top + jnp.log(total))
    share = f_full.shape[0] // lax.axis_size("col")
    f_out = lax.dynamic_slice_in_dim(f_full, lax.axis_index("col") * share, share)
    fblocks = f_full.reshape(group_rows, GROUP_WIDTH, BLOCK_CELLS)

    def col_stats(args):
        xb, fb, chosen = args
        cost = pair_cost(xb, yblocks[chosen])
        score = (fb[:, None, :, None] - cost) / EPSILON
        peak_value = jnp.max(score, axis=2)
        mass_weights = jnp.sum(jnp.exp(score - peak_value[:, :, None, :]), axis=2)
        return (peak_value, mass_weights)

    peak_value, mass_weights = lax.map(col_stats, (cross_blocks, fblocks, ids_grouped))
    peak_value = peak_value.reshape(sparse_block_rows, slot_table, BLOCK_CELLS)
    mass_weights = mass_weights.reshape(sparse_block_rows, slot_table, BLOCK_CELLS)
    target_ids = jnp.arange(tbc, dtype=jnp.int32)
    hit = (cell_index[:, :, None] == target_ids[None, None, :]) & valid[:, :, None]
    local_best = jnp.max(jnp.where(hit[..., None], peak_value[:, :, None, :], NEG), axis=(0, 1))
    lift = jnp.where(hit[..., None], peak_value[:, :, None, :] - local_best[None, None], NEG)
    best, summed = combined_all(
        (local_best, jnp.sum(mass_weights[:, :, None, :] * jnp.exp(lift), axis=(0, 1))),
        "row",
        combine,
    )
    g_out = EPSILON * log_b - EPSILON * (best + jnp.log(summed)).reshape(-1)
    return (f_out, g_out)


def solution(mesh):
    in_specs = (
        P(None, ("row", "col")),
        P(None, "col"),
        P(("row", "col")),
        P("col"),
        P("col"),
        P("row", "col", None),
        P("row", "col"),
    )
    out_specs = (P(("row", "col")), P("col"))
    return jax.shard_map(
        per_device, mesh=mesh, in_specs=in_specs, out_specs=out_specs, check_vma=False
    )
```

profile of v0, /device:TPU:1, one launch (start us, length us, event | category | flops | bytes accessed | tf_op | source)
XLA Modules:
  0.0 497.6 jit_solution(15408323692563191677)
XLA Ops:
  12.6 50.8 %all-gather.8.cloned.1.call-done = f32[32,16384]{1,0:T(8,128)} async-done(((f32[32,1024]{1,0:T(8,128)}), f32[32,16384]{1,0:T(8,128)}) %all-gather.8.cloned.1.call-update) | async-done | bytes 2097168 | tf_op jit(solution)/shard_map/all_gather | solution.py:41
  65.3 138.4 %while.48 = (s32[]{:T(128)}, f32[16,4,256]{2,1,0:T(4,128)S(1)}, f32[16,4,256]{2,1,0:T(4,128)S(1)}, pred[16,4,4]{2,1,0:T(4,128)(4,1)S(1)}, s32[16,4,4]{2,1,0:T(4,...) while((s32[]{:T(128)}, f32[16,4,256]{2,1,0:T(4,128)S(1)}, ...), condition=%wide.region_5.6_spmd, body=%wide.region_0.5_spmd.sunk | while | flops 418703424 | bytes 10941545 | solution.py:68
  66.7 5.4 %fusion.31 = (f32[4,256]{1,0:T(4,128)S(1)}, f32[4,4,256,256]{3,2,1,0:T(8,128)S(1)}) fusion(f32[4,4,256]{2,1,0:T(4,128)S(1)} %multiply_reduce_fusion.5, f32[4,256]{1,0:T(4,128)S(1)} %fusion.30, f32[4,4,256]{2,1,0:T(4,128)S(1)} %reshape.205, pred[4,4]{1,0:T(4,128)(4,1)S(1)} %dynamic-slice_bitcast_fusion.4, f32[4,4,32,256]{3,2,1,0:T(8,128)S(1)} %bitcast.157, ...), kind=kOutput, calls=%fused_computation.16.clone.1 | convolution fusion | flops 409992192 | bytes 4891140 | tf_op jit(solution)/shard_map/while/body/eval_jaxpr/gli,gelj->geij/dot_general | solution.py:23
  75.4 5.4 %fusion.31 = (f32[4,256]{1,0:T(4,128)S(1)}, f32[4,4,256,256]{3,2,1,0:T(8,128)S(1)}) fusion(f32[4,4,256]{2,1,0:T(4,128)S(1)} %multiply_reduce_fusion.5, f32[4,256]{1,0:T(4,128)S(1)} %fusion.30, f32[4,4,256]{2,1,0:T(4,128)S(1)} %reshape.205, pred[4,4]{1,0:T(4,128)(4,1)S(1)} %dynamic-slice_bitcast_fusion.4, f32[4,4,32,256]{3,2,1,0:T(8,128)S(1)} %bitcast.157, ...), kind=kOutput, calls=%fused_computation.16.clone.1 | convolution fusion | flops 409992192 | bytes 4891140 | tf_op jit(solution)/shard_map/while/body/eval_jaxpr/gli,gelj->geij/dot_general | solution.py:23
  84.0 5.4 %fusion.31 = (f32[4,256]{1,0:T(4,128)S(1)}, f32[4,4,256,256]{3,2,1,0:T(8,128)S(1)}) fusion(f32[4,4,256]{2,1,0:T(4,128)S(1)} %multiply_reduce_fusion.5, f32[4,256]{1,0:T(4,128)S(1)} %fusion.30, f32[4,4,256]{2,1,0:T(4,128)S(1)} %reshape.205, pred[4,4]{1,0:T(4,128)(4,1)S(1)} %dynamic-slice_bitcast_fusion.4, f32[4,4,32,256]{3,2,1,0:T(8,128)S(1)} %bitcast.157, ...), kind=kOutput, calls=%fused_computation.16.clone.1 | convolution fusion | flops 409992192 | bytes 4891140 | tf_op jit(solution)/shard_map/while/body/eval_jaxpr/gli,gelj->geij/dot_general | solution.py:23
  92.7 5.4 %fusion.31 = (f32[4,256]{1,0:T(4,128)S(1)}, f32[4,4,256,256]{3,2,1,0:T(8,128)S(1)}) fusion(f32[4,4,256]{2,1,0:T(4,128)S(1)} %multiply_reduce_fusion.5, f32[4,256]{1,0:T(4,128)S(1)} %fusion.30, f32[4,4,256]{2,1,0:T(4,128)S(1)} %reshape.205, pred[4,4]{1,0:T(4,128)(4,1)S(1)} %dynamic-slice_bitcast_fusion.4, f32[4,4,32,256]{3,2,1,0:T(8,128)S(1)} %bitcast.157, ...), kind=kOutput, calls=%fused_computation.16.clone.1 | convolution fusion | flops 409992192 | bytes 4891140 | tf_op jit(solution)/shard_map/while/body/eval_jaxpr/gli,gelj->geij/dot_general | solution.py:23
  101.3 5.4 %fusion.31 = (f32[4,256]{1,0:T(4,128)S(1)}, f32[4,4,256,256]{3,2,1,0:T(8,128)S(1)}) fusion(f32[4,4,256]{2,1,0:T(4,128)S(1)} %multiply_reduce_fusion.5, f32[4,256]{1,0:T(4,128)S(1)} %fusion.30, f32[4,4,256]{2,1,0:T(4,128)S(1)} %reshape.205, pred[4,4]{1,0:T(4,128)(4,1)S(1)} %dynamic-slice_bitcast_fusion.4, f32[4,4,32,256]{3,2,1,0:T(8,128)S(1)} %bitcast.157, ...), kind=kOutput, calls=%fused_computation.16.clone.1 | convolution fusion | flops 409992192 | bytes 4891140 | tf_op jit(solution)/shard_map/while/body/eval_jaxpr/gli,gelj->geij/dot_general | solution.py:23
  110.0 5.4 %fusion.31 = (f32[4,256]{1,0:T(4,128)S(1)}, f32[4,4,256,256]{3,2,1,0:T(8,128)S(1)}) fusion(f32[4,4,256]{2,1,0:T(4,128)S(1)} %multiply_reduce_fusion.5, f32[4,256]{1,0:T(4,128)S(1)} %fusion.30, f32[4,4,256]{2,1,0:T(4,128)S(1)} %reshape.205, pred[4,4]{1,0:T(4,128)(4,1)S(1)} %dynamic-slice_bitcast_fusion.4, f32[4,4,32,256]{3,2,1,0:T(8,128)S(1)} %bitcast.157, ...), kind=kOutput, calls=%fused_computation.16.clone.1 | convolution fusion | flops 409992192 | bytes 4891140 | tf_op jit(solution)/shard_map/while/body/eval_jaxpr/gli,gelj->geij/dot_general | solution.py:23
  118.6 5.4 %fusion.31 = (f32[4,256]{1,0:T(4,128)S(1)}, f32[4,4,256,256]{3,2,1,0:T(8,128)S(1)}) fusion(f32[4,4,256]{2,1,0:T(4,128)S(1)} %multiply_reduce_fusion.5, f32[4,256]{1,0:T(4,128)S(1)} %fusion.30, f32[4,4,256]{2,1,0:T(4,128)S(1)} %reshape.205, pred[4,4]{1,0:T(4,128)(4,1)S(1)} %dynamic-slice_bitcast_fusion.4, f32[4,4,32,256]{3,2,1,0:T(8,128)S(1)} %bitcast.157, ...), kind=kOutput, calls=%fused_computation.16.clone.1 | convolution fusion | flops 409992192 | bytes 4891140 | tf_op jit(solution)/shard_map/while/body/eval_jaxpr/gli,gelj->geij/dot_general | solution.py:23
  127.3 5.4 %fusion.31 = (f32[4,256]{1,0:T(4,128)S(1)}, f32[4,4,256,256]{3,2,1,0:T(8,128)S(1)}) fusion(f32[4,4,256]{2,1,0:T(4,128)S(1)} %multiply_reduce_fusion.5, f32[4,256]{1,0:T(4,128)S(1)} %fusion.30, f32[4,4,256]{2,1,0:T(4,128)S(1)} %reshape.205, pred[4,4]{1,0:T(4,128)(4,1)S(1)} %dynamic-slice_bitcast_fusion.4, f32[4,4,32,256]{3,2,1,0:T(8,128)S(1)} %bitcast.157, ...), kind=kOutput, calls=%fused_computation.16.clone.1 | convolution fusion | flops 409992192 | bytes 4891140 | tf_op jit(solution)/shard_map/while/body/eval_jaxpr/gli,gelj->geij/dot_general | solution.py:23
  135.9 5.4 %fusion.31 = (f32[4,256]{1,0:T(4,128)S(1)}, f32[4,4,256,256]{3,2,1,0:T(8,128)S(1)}) fusion(f32[4,4,256]{2,1,0:T(4,128)S(1)} %multiply_reduce_fusion.5, f32[4,256]{1,0:T(4,128)S(1)} %fusion.30, f32[4,4,256]{2,1,0:T(4,128)S(1)} %reshape.205, pred[4,4]{1,0:T(4,128)(4,1)S(1)} %dynamic-slice_bitcast_fusion.4, f32[4,4,32,256]{3,2,1,0:T(8,128)S(1)} %bitcast.157, ...), kind=kOutput, calls=%fused_computation.16.clone.1 | convolution fusion | flops 409992192 | bytes 4891140 | tf_op jit(solution)/shard_map/while/body/eval_jaxpr/gli,gelj->geij/dot_general | solution.py:23
  144.6 5.4 %fusion.31 = (f32[4,256]{1,0:T(4,128)S(1)}, f32[4,4,256,256]{3,2,1,0:T(8,128)S(1)}) fusion(f32[4,4,256]{2,1,0:T(4,128)S(1)} %multiply_reduce_fusion.5, f32[4,256]{1,0:T(4,128)S(1)} %fusion.30, f32[4,4,256]{2,1,0:T(4,128)S(1)} %reshape.205, pred[4,4]{1,0:T(4,128)(4,1)S(1)} %dynamic-slice_bitcast_fusion.4, f32[4,4,32,256]{3,2,1,0:T(8,128)S(1)} %bitcast.157, ...), kind=kOutput, calls=%fused_computation.16.clone.1 | convolution fusion | flops 409992192 | bytes 4891140 | tf_op jit(solution)/shard_map/while/body/eval_jaxpr/gli,gelj->geij/dot_general | solution.py:23
  153.2 5.4 %fusion.31 = (f32[4,256]{1,0:T(4,128)S(1)}, f32[4,4,256,256]{3,2,1,0:T(8,128)S(1)}) fusion(f32[4,4,256]{2,1,0:T(4,128)S(1)} %multiply_reduce_fusion.5, f32[4,256]{1,0:T(4,128)S(1)} %fusion.30, f32[4,4,256]{2,1,0:T(4,128)S(1)} %reshape.205, pred[4,4]{1,0:T(4,128)(4,1)S(1)} %dynamic-slice_bitcast_fusion.4, f32[4,4,32,256]{3,2,1,0:T(8,128)S(1)} %bitcast.157, ...), kind=kOutput, calls=%fused_computation.16.clone.1 | convolution fusion | flops 409992192 | bytes 4891140 | tf_op jit(solution)/shard_map/while/body/eval_jaxpr/gli,gelj->geij/dot_general | solution.py:23
  161.9 5.4 %fusion.31 = (f32[4,256]{1,0:T(4,128)S(1)}, f32[4,4,256,256]{3,2,1,0:T(8,128)S(1)}) fusion(f32[4,4,256]{2,1,0:T(4,128)S(1)} %multiply_reduce_fusion.5, f32[4,256]{1,0:T(4,128)S(1)} %fusion.30, f32[4,4,256]{2,1,0:T(4,128)S(1)} %reshape.205, pred[4,4]{1,0:T(4,128)(4,1)S(1)} %dynamic-slice_bitcast_fusion.4, f32[4,4,32,256]{3,2,1,0:T(8,128)S(1)} %bitcast.157, ...), kind=kOutput, calls=%fused_computation.16.clone.1 | convolution fusion | flops 409992192 | bytes 4891140 | tf_op jit(solution)/shard_map/while/body/eval_jaxpr/gli,gelj->geij/dot_general | solution.py:23
  170.5 5.4 %fusion.31 = (f32[4,256]{1,0:T(4,128)S(1)}, f32[4,4,256,256]{3,2,1,0:T(8,128)S(1)}) fusion(f32[4,4,256]{2,1,0:T(4,128)S(1)} %multiply_reduce_fusion.5, f32[4,256]{1,0:T(4,128)S(1)} %fusion.30, f32[4,4,256]{2,1,0:T(4,128)S(1)} %reshape.205, pred[4,4]{1,0:T(4,128)(4,1)S(1)} %dynamic-slice_bitcast_fusion.4, f32[4,4,32,256]{3,2,1,0:T(8,128)S(1)} %bitcast.157, ...), kind=kOutput, calls=%fused_computation.16.clone.1 | convolution fusion | flops 409992192 | bytes 4891140 | tf_op jit(solution)/shard_map/while/body/eval_jaxpr/gli,gelj->geij/dot_general | solution.py:23
  179.2 5.4 %fusion.31 = (f32[4,256]{1,0:T(4,128)S(1)}, f32[4,4,256,256]{3,2,1,0:T(8,128)S(1)}) fusion(f32[4,4,256]{2,1,0:T(4,128)S(1)} %multiply_reduce_fusion.5, f32[4,256]{1,0:T(4,128)S(1)} %fusion.30, f32[4,4,256]{2,1,0:T(4,128)S(1)} %reshape.205, pred[4,4]{1,0:T(4,128)(4,1)S(1)} %dynamic-slice_bitcast_fusion.4, f32[4,4,32,256]{3,2,1,0:T(8,128)S(1)} %bitcast.157, ...), kind=kOutput, calls=%fused_computation.16.clone.1 | convolution fusion | flops 409992192 | bytes 4891140 | tf_op jit(solution)/shard_map/while/body/eval_jaxpr/gli,gelj->geij/dot_general | solution.py:23
  187.8 5.4 %fusion.31 = (f32[4,256]{1,0:T(4,128)S(1)}, f32[4,4,256,256]{3,2,1,0:T(8,128)S(1)}) fusion(f32[4,4,256]{2,1,0:T(4,128)S(1)} %multiply_reduce_fusion.5, f32[4,256]{1,0:T(4,128)S(1)} %fusion.30, f32[4,4,256]{2,1,0:T(4,128)S(1)} %reshape.205, pred[4,4]{1,0:T(4,128)(4,1)S(1)} %dynamic-slice_bitcast_fusion.4, f32[4,4,32,256]{3,2,1,0:T(8,128)S(1)} %bitcast.157, ...), kind=kOutput, calls=%fused_computation.16.clone.1 | convolution fusion | flops 409992192 | bytes 4891140 | tf_op jit(solution)/shard_map/while/body/eval_jaxpr/gli,gelj->geij/dot_general | solution.py:23
  196.5 5.4 %fusion.31 = (f32[4,256]{1,0:T(4,128)S(1)}, f32[4,4,256,256]{3,2,1,0:T(8,128)S(1)}) fusion(f32[4,4,256]{2,1,0:T(4,128)S(1)} %multiply_reduce_fusion.5, f32[4,256]{1,0:T(4,128)S(1)} %fusion.30, f32[4,4,256]{2,1,0:T(4,128)S(1)} %reshape.205, pred[4,4]{1,0:T(4,128)(4,1)S(1)} %dynamic-slice_bitcast_fusion.4, f32[4,4,32,256]{3,2,1,0:T(8,128)S(1)} %bitcast.157, ...), kind=kOutput, calls=%fused_computation.16.clone.1 | convolution fusion | flops 409992192 | bytes 4891140 | tf_op jit(solution)/shard_map/while/body/eval_jaxpr/gli,gelj->geij/dot_general | solution.py:23
  205.3 19.4 %all_gather.24 = f32[16384]{0:T(1024)} all-gather(f32[1024]{0:T(1024)S(1)} %copy-done.4), channel_id=1, replica_groups=mesh['row'=16,'col'=16] {'col'}, dimensions={0}, use_global_device_ids=true | all-gather | bytes 69632 | tf_op jit(solution)/shard_map/all_gather | solution.py:42
  225.6 25.5 %all-gather.10.cloned.1.call-done = f32[16,1,16384]{2,1,0:T(1,128)} async-done(((f32[1,1,16384]{2,1,0:T(1,128)}), f32[16,1,16384]{2,1,0:T(1,128)}) %all-gather.10.cloned.1.call-update) | async-done | bytes 1048592 | tf_op jit(solution)/shard_map/all_gather | solution.py:15
  253.0 47.6 %all-gather.12.cloned.1.call-done = f32[16,1,16384]{2,1,0:T(1,128)} async-done(((f32[1,1,16384]{2,1,0:T(1,128)}), f32[16,1,16384]{2,1,0:T(1,128)}) %all-gather.12.cloned.1.call-update) | async-done | bytes 1048592 | tf_op jit(solution)/shard_map/all_gather | solution.py:15
  303.5 18.4 %while.49 = (s32[]{:T(128)}, f32[16384]{0:T(1024)S(1)}, f32[16384]{0:T(1024)S(1)}, f32[15,16384]{1,0:T(8,128)S(1)}, f32[15,16384]{1,0:T(8,128)}, /*index=5*/s32[]{:T(128)}) while((s32[]{:T(128)}, f32[16384]{0:T(1024)S(1)}, f32[16384]{0:T(1024)S(1)}, f32[15,16384]{1,0:T(8,128)S(1)}, f32[15,16384]{1,0:T(8,128)}, /*index=5*/s32[]{:T(128)}) %tuple.112), condition=%wide.region_7.8_spmd, body=%wide.region_6.7_spmd.sunk | while | flops 98306 | bytes 655441 | solution.py:18
  322.8 128.4 %while.50 = (s32[]{:T(128)}, f32[16,4,4,256]{3,2,1,0:T(4,128)}, f32[16,4,4,256]{3,2,1,0:T(4,128)}, f32[16,4,256]{2,1,0:T(4,128)S(1)}, f32[16,4,32,256]{3,2,1,0:T...) while((s32[]{:T(128)}, f32[16,4,4,256]{3,2,1,0:T(4,128)}, ...), condition=%wide.region_13.14_spmd, body=%wide.region_8.13_spmd.sunk | while | flops 416600128 | bytes 10945009 | solution.py:85
  324.3 4.3 fusion.34
  332.3 4.3 fusion.34
  340.3 4.3 fusion.34
  372.4 4.3 fusion.34
  380.5 4.3 fusion.34
  396.5 4.3 fusion.34
  428.6 4.3 fusion.34
  452.5 19.7 %all-gather = f32[128,256]{1,0:T(8,128)S(1)} all-gather(f32[8,256]{1,0:T(8,128)S(1)} %select_reduce_fusion), channel_id=2, replica_groups=mesh['row'=16,'col'=16] {'row'}, dimensions={0}, use_global_device_ids=true | all-gather | bytes 139264 | tf_op jit(solution)/shard_map/all_gather | solution.py:15
  473.9 15.3 %all-gather.1 = f32[128,256]{1,0:T(8,128)S(1)} all-gather(f32[8,256]{1,0:T(8,128)S(1)} %multiply_reduce_fusion.2), channel_id=3, replica_groups=mesh['row'=16,'col'=16] {'row'}, dimensions={0}, use_global_device_ids=true | all-gather | bytes 139264 | tf_op jit(solution)/shard_map/all_gather | solution.py:15
  (431 shorter events, 187.0 us)
Async XLA Ops:
  7.2 56.2 %all-gather.8.cloned.1.call-start = ((), (), s32[]{:S(2)}) async-start(), calls=%async_computation | async-start | bytes 2228224 | tf_op jit(solution)/shard_map/all_gather | solution.py:41
  7.9 243.2 %all-gather.10.cloned.1.call-start = ((), (), s32[]{:S(2)}) async-start(), calls=%async_computation.1 | async-start | bytes 1114112 | tf_op jit(solution)/shard_map/all_gather | solution.py:15
  65.3 139.9 %copy-start.3 = (s32[64,1,4]{0,2,1:T(4,128)S(1)}, s32[64,1,4]{0,2,1:T(4,128)}, u32[]{:S(2)}) copy-start(s32[64,1,4]{0,2,1:T(4,128)} %param.20) | copy-start | bytes 3076
  65.3 140.0 %copy-start.4 = (f32[1024]{0:T(1024)S(1)}, f32[1024]{0:T(1024)}, u32[]{:S(2)}) copy-start(f32[1024]{0:T(1024)} %param.17) | copy-start | bytes 12292
  65.3 159.4 %copy-start.5 = (s32[64,1]{0,1:T(1,128)S(1)}, s32[64,1]{0,1:T(1,128)}, u32[]{:S(2)}) copy-start(s32[64,1]{0,1:T(1,128)} %param.21) | copy-start | bytes 772
  203.7 47.4 %copy-start.1 = (s32[16,4,4]{2,1,0:T(4,128)}, s32[16,4,4]{2,1,0:T(4,128)S(1)}, u32[]{:S(2)}) copy-start(s32[16,4,4]{2,1,0:T(4,128)S(1)} %get-tuple-element.539) | copy-start | bytes 3076
  204.4 96.2 %all-gather.12.cloned.1.call-start = ((), (), s32[]{:S(2)}) async-start(), calls=%async_computation.2 | async-start | bytes 1114112 | tf_op jit(solution)/shard_map/all_gather | solution.py:15
  251.1 52.4 %slice-start = ((f32[16,1,16384]{2,1,0:T(1,128)}), f32[1,1,16384]{2,1,0:T(1,128)S(1)}, s32[]{:S(2)}) async-start(f32[16,1,16384]{2,1,0:T(1,128)} %all-gather.10.cloned.1.call-done), calls=%async_computation.3 | async-start | bytes 131072 | tf_op jit(solution)/shard_map/slice | solution.py:16
  300.6 2.9 slice-start.1
  322.8 128.4 %copy-start = (pred[64,4,8]{2,1,0:T(4,128)(4,1)S(1)}, pred[64,4,8]{2,1,0:T(4,128)(4,1)}, u32[]{:S(2)}) copy-start(pred[64,4,8]{2,1,0:T(4,128)(4,1)} %fusion.19) | copy-start | bytes 6148
  322.8 167.6 %copy-start.2 = (f32[2048]{0:T(1024)S(1)}, f32[2048]{0:T(1024)}, u32[]{:S(2)}) copy-start(f32[2048]{0:T(1024)} %param.18) | copy-start | bytes 24580
Sparse Core Ops, SparseCore 0:
  10.4 52.8 all-gather.7
  204.5 46.5 all-gather.9
  253.6 47.0 all-gather.11
where the time goes:
time: 499 us; the launch traced here: 498 us
  matrix products  155 us (31%)
  waiting for transfers between devices  125 us (25%)
  other arithmetic  77.2 us (15%)
  local copies, waits for them, and re-layouts  70.2 us (14%)
  blocking collectives  54.5 us (11%)
  between operations  14 us (3%)
    dot_general x32, matrix products, pair_cost(): jnp.einsum('gli,gelj->geij', xb, yb, precision=lax.Precision.HIGHEST)  155 us
    all_gather x2, waiting for transfers between devices, combined_all(): pieces = jax.tree.map(lambda part: lax.all_gather(part, axis), value)  73.1 us
    all_gather x1, waiting for transfers between devices, per_device(): lax.all_gather(src_emb, 'col', axis=1, tiled=True)  50.8 us
    all_gather x2, blocking collectives, combined_all(): pieces = jax.tree.map(lambda part: lax.all_gather(part, axis), value)  35.1 us
    reduce_sum x16, other arithmetic, row_stats(): total = jnp.sum(jnp.exp(score - top[:, None, :, None]), axis=(1, 3))  28.1 us
    reduce_sum x16, other arithmetic, col_stats(): mass_weights = jnp.sum(jnp.exp(score - peak_value[:, :, None, :]), axis=2)  26.5 us
    all_gather x1, blocking collectives, per_device(): lax.all_gather(log_a, 'col', axis=0, tiled=True)  19.4 us
    dynamic_slice x15, local copies, waits for them, and re-layouts, combined_all(): lax.scan(lambda subtotal, piece: (join(subtotal, piece), None), head, tail)  17.1 us
  transfers between devices with their start and end apart: 3, of which 3 were waited for; matrix products, arithmetic and copies ran while one was open for 2% of the time, Pallas kernels for 0%

commit v1 on v0

v1 whole, which is shorter than its diff:
```python
import functools

import jax
import jax.numpy as jnp
from jax import lax
from jax.experimental import pallas as pl
from jax.experimental.pallas import tpu as pltpu
from jax.sharding import PartitionSpec as P

MESH = pl.DeviceIdType.MESH
LAT = 32
BC = 256
TBC = 8
KC = 4
SIDE = 4
ROWS = 16
SBD = 4
NOSLOT = 8
NEG = -1e30
EPSILON = 2.0
LOG2E = 1.4426950408889634
LN2 = 0.6931471805599453
KAPPA = LOG2E / EPSILON
OFFSETS = (0, 1, 3, 2)
THERE = (0, 2, 1, 3)
STORED = 3 * SIDE * SBD * KC


def split3(v):
    hi = v.astype(jnp.bfloat16)
    rest = v - hi.astype(jnp.float32)
    mid = rest.astype(jnp.bfloat16)
    low = (rest - mid.astype(jnp.float32)).astype(jnp.bfloat16)
    return hi, mid, low


def bias_rows(first, second):
    row = lax.broadcasted_iota(jnp.int32, (LAT, BC), 0)
    out = jnp.zeros((LAT, BC), jnp.float32)
    for k, v in enumerate(tuple(first) + tuple(second)):
        v = 1.0 if v is None else v.astype(jnp.float32)
        out = jnp.where(row == k, v, out)
    return out.astype(jnp.bfloat16)


def gray(i):
    return i + i // 2 - 2 * (i // 3)


def kernel(
    x_ref, y_ref, la_ref, g_ref, lb_ref, ids_ref, f_ref, gp_ref,
    xg, yg, lag, gg, idg, ids, lhs, rhs, mrow, srow, keep, tile, part, uall, cm, cs, idv, cpart, rpart,
    xs_s, xs_r, ys_s, ys_r, yf_s, yf_r, la_s, la_r, g_s, g_r, id_s, id_r, ex_s, ex_r, cy_s, cy_r, rr_s, rr_r, loc,
):
    row = lax.axis_index("row")
    col = lax.axis_index("col")
    yme, xme = col // SIDE, col % SIDE
    core = row % 2
    half = LAT // 2
    sibling = (row + 1 - 2 * core, col)

    def xpeer(i):
        return (row, yme * SIDE + (xme + OFFSETS[i]) % SIDE)

    def ypeer(i):
        return (row, ((yme + OFFSETS[i]) % SIDE) * SIDE + xme)

    def rpeer(o):
        return ((row + o) % ROWS, col)

    barrier = pltpu.get_barrier_semaphore()
    for i in range(1, SIDE):
        pl.semaphore_signal(barrier, inc=1, device_id=xpeer(i), device_id_type=MESH)
        pl.semaphore_signal(barrier, inc=1, device_id=ypeer(i), device_id_type=MESH)
    for o in range(1, ROWS):
        pl.semaphore_signal(barrier, inc=1, device_id=rpeer(o), device_id_type=MESH)

    xg[0] = x_ref[...]
    yg[0] = y_ref[...]
    lag[xme] = la_ref[...]
    gg[0] = g_ref[...]
    idg[0] = ids_ref[yme]

    rhs[SIDE * TBC] = jnp.concatenate(
        [jnp.zeros((96, BC), jnp.bfloat16)]
        + [bias_rows([None] * 3, [jnp.full((1, BC), NEG, jnp.float32)] + [jnp.zeros((1, BC), jnp.float32)] * 2)]
        + [jnp.zeros((128, BC), jnp.bfloat16)], axis=0)

    def init(b, _):
        mrow[b] = jnp.full((BC, 128), NEG, jnp.float32)
        srow[b] = jnp.zeros((BC, 128), jnp.float32)
        return 0

    lax.fori_loop(0, SIDE * SBD, init, 0)

    pl.semaphore_wait(barrier, 2 * (SIDE - 1) + ROWS - 1)

    def remote(src, dst, s, r, dev):
        return pltpu.make_async_remote_copy(
            src_ref=src, dst_ref=dst, send_sem=s, recv_sem=r, device_id=dev, device_id_type=MESH)

    mine = pl.ds(pl.multiple_of(core * half, half), half)
    theirs = pl.ds(pl.multiple_of((1 - core) * half, half), half)
    sends = []

    def send(src, dst, s, r, dev):
        copy = remote(src, dst, s, r, dev)
        copy.start()
        sends.append(copy)

    for i in range(1, SIDE):
        t = THERE[i]
        send(x_ref, xg.at[t], xs_s.at[t], xs_r.at[t], xpeer(i))
        send(y_ref.at[mine], yg.at[t, mine], ys_s.at[t], ys_r.at[t], ypeer(i))
        send(ids_ref.at[(yme + OFFSETS[i]) % SIDE], idg.at[t], id_s.at[t], id_r.at[t], ypeer(i))
        send(g_ref, gg.at[t], g_s.at[t], g_r.at[t], ypeer(i))
        send(la_ref, lag.at[xme], la_s.at[t], la_r.at[t], xpeer(i))

    def await_x(i):
        remote(x_ref, xg.at[i], xs_s.at[i], xs_r.at[i], sibling).wait_recv()

    def forward_y(i):
        remote(y_ref.at[mine], yg.at[i, mine], ys_s.at[i], ys_r.at[i], sibling).wait_recv()
        remote(yg.at[i, mine], yg.at[i, mine], yf_s.at[i], yf_r.at[i], sibling).start()

    def await_y(i):
        remote(yg.at[i, mine], yg.at[i, theirs], yf_s.at[i], yf_r.at[i], sibling).wait()
        remote(g_ref, gg.at[i], g_s.at[i], g_r.at[i], sibling).wait_recv()
        remote(ids_ref.at[0], idg.at[i], id_s.at[i], id_r.at[i], sibling).wait_recv()

    def prep_x(i):
        def one(b, _):
            v = xg[i, :, pl.ds(pl.multiple_of(b * BC, BC), BC)]
            hi, mid, low = split3(v * KAPPA)
            norm = jnp.sum(v * v, axis=0, keepdims=True) * (-0.5 * KAPPA)
            z = jnp.concatenate(
                [hi, mid, low, bias_rows(split3(norm), [None] * 3), hi, mid, hi, jnp.zeros((LAT, BC), jnp.bfloat16)], axis=0)
            lhs[i * SBD + b] = z.T
            return 0

        lax.fori_loop(0, SBD, one, 0)

    def prep_y(i):
        def one(t, _):
            v = yg[i, :, pl.ds(pl.multiple_of(t * BC, BC), BC)]
            hi, mid, low = split3(v)
            bias = gg[i, pl.ds(t, 1), :] * KAPPA - jnp.sum(v * v, axis=0, keepdims=True) * (0.5 * KAPPA)
            rhs[i * TBC + t] = jnp.concatenate(
                [hi, hi, hi, bias_rows([None] * 3, split3(bias)), mid, mid, low, jnp.zeros((LAT, BC), jnp.bfloat16)], axis=0)
            return 0

        lax.fori_loop(0, TBC, one, 0)
        copy = pltpu.make_async_copy(idg.at[i], ids.at[i], loc)
        copy.start()
        copy.wait()

    def listed(xi, yi, b, k):
        return ids[yi, 0, (((xme + gray(xi)) % SIDE) * SBD + b) * KC + k]

    def score(xi, yi, b, k):
        t = listed(xi, yi, b, k)
        t = jnp.where(t == NOSLOT, SIDE * TBC, yi * TBC + t)
        return jnp.dot(lhs[xi * SBD + b], rhs[t], preferred_element_type=jnp.float32)

    def row_step(xi, yi, kept):
        for b in range(SBD):
            j = xi * SBD + b
            tiles = []
            for k in range(KC):
                v = score(xi, yi, b, k)
                if kept:
                    keep[(yi * SIDE + xi) * SBD * KC + b * KC + k] = v
                tiles.append(v)
            old = mrow[j]
            top = old
            for v in tiles:
                top = jnp.maximum(top, jnp.maximum(v[:, :128], v[:, 128:]))
            total = srow[j] * jnp.exp2(old - top)
            for v in tiles:
                total = total + (jnp.exp2(v[:, :128] - top) + jnp.exp2(v[:, 128:] - top))
            mrow[j] = top
            srow[j] = total

    def first(s, _):
        early = s < 9
        xi = jnp.where(early, s % 3, SIDE - 1)
        yi = jnp.where(early, s // 3, s - 9)

        @pl.when((s == 1) | (s == 2) | (s == 9))
        def _():
            await_x(xi)

        @pl.when(s == 1)
        def _():
            forward_y(1)
            forward_y(2)

        @pl.when(s == 9)
        def _():
            forward_y(3)

        @pl.when((s == 3) | (s == 6))
        def _():
            await_y(yi)

        @pl.when((s < 3) | (s == 9))
        def _():
            prep_x(xi)

        @pl.when((s == 0) | (s == 3) | (s == 6))
        def _():
            prep_y(yi)

        row_step(xi, yi, True)
        return 0

    lax.fori_loop(0, 12, first, 0)
    await_y(3)
    prep_y(3)

    def second(xi, _):
        row_step(xi, SIDE - 1, False)
        return 0

    lax.fori_loop(0, SIDE, second, 0)

    lane = lax.broadcasted_iota(jnp.int32, (BC, 128), 1)
    tile[...] = jnp.zeros((BC, 128), jnp.float32)

    def reduce_rows(j, _):
        m = mrow[j]
        top = jnp.max(m, axis=1, keepdims=True)
        total = jnp.sum(srow[j] * jnp.exp2(m - top), axis=1, keepdims=True)
        place = ((xme + gray(j // SBD)) % SIDE) * SBD + j % SBD
        tile[...] = jnp.where(lane == place, top + jnp.log2(total), tile[...])
        return 0

    lax.fori_loop(0, SIDE * SBD, reduce_rows, 0)
    part[0] = tile[...].T[: SIDE * SBD]

    for i in range(1, SIDE):
        t = THERE[i]
        send(part.at[0], part.at[t], ex_s.at[t], ex_r.at[t], xpeer(i))
    for i in range(1, SIDE):
        remote(part.at[0], part.at[i], ex_s.at[i], ex_r.at[i], sibling).wait_recv()
        remote(la_ref, lag.at[0], la_s.at[i], la_r.at[i], sibling).wait_recv()

    parts = [part[i] for i in range(SIDE)]
    top = functools.reduce(jnp.maximum, parts)
    lse = top + jnp.log2(sum(jnp.exp2(v - top) for v in parts))
    mass = jnp.concatenate([lag[a, :SBD] for a in range(SIDE)], axis=0)
    u = mass * LOG2E - lse
    for a in range(SIDE):
        uall[a] = u[a * SBD:(a + 1) * SBD] * (EPSILON * LN2)
    f_ref[...] = uall[xme]
    tile[...] = jnp.concatenate([u, jnp.zeros((128 - SIDE * SBD, BC), jnp.float32)], axis=0).T

    def spread(j, _):
        place = ((xme + gray(j // SBD)) % SIDE) * SBD + j % SBD
        c = jnp.sum(jnp.where(lane == place, tile[...], 0.0), axis=1, keepdims=True)
        mrow[j] = jnp.broadcast_to(c, (BC, 128))
        return 0

    lax.fori_loop(0, SIDE * SBD, spread, 0)

    def col_step(xi, yi, kept):
        for b in range(SBD):
            for k in range(KC):
                if kept:
                    v = keep.at[(yi * SIDE + xi) * SBD * KC + b * KC + k]
                else:
                    v = score(xi, yi, b, k)
                at = b * KC + k
                for h in range(2):
                    lanes = slice(h * 128, (h + 1) * 128)
                    t = (v[:, lanes] + mrow[xi * SBD + b]).reshape(BC // 8, 8, 128)
                    peak = jnp.max(jnp.max(t, axis=0), axis=0, keepdims=True)
                    total = jnp.sum(jnp.sum(jnp.exp2(t - peak), axis=0), axis=0, keepdims=True)
                    cm[yi * SIDE + xi, at:at + 1, lanes] = peak
                    cs[yi * SIDE + xi, at:at + 1, lanes] = total
                idv[yi * SIDE + xi, at:at + 1, :] = jnp.full((1, BC), listed(xi, yi, b, k), jnp.int32)

    def finish_cols(yi):
        group = pl.ds(yi * SIDE, SIDE)
        for t in range(TBC):
            hit = idv[group] == t
            m = cm[group]
            peak = jnp.max(jnp.where(hit, m, NEG).reshape(-1, BC), axis=0, keepdims=True)
            total = jnp.where(hit, cs[group] * jnp.exp2(m - peak[None]), 0.0)
            total = jnp.sum(total.reshape(-1, BC), axis=0, keepdims=True)
            some = total > 0.0
            cpart[yi, t:t + 1, :] = jnp.where(some, peak + jnp.log2(jnp.where(some, total, 1.0)), NEG)

    def third(xi, _):
        col_step(xi, SIDE - 1, False)
        return 0

    lax.fori_loop(0, SIDE, third, 0)
    finish_cols(SIDE - 1)
    send(cpart.at[3], rpart.at[0, THERE[3]], cy_s.at[3], cy_r.at[THERE[3]], ypeer(3))

    def fourth(yi):
        def body(xi, _):
            col_step(xi, yi, True)
            return 0

        lax.fori_loop(0, SIDE, body, 0)
        finish_cols(yi)

    def fourth_pair(q, _):
        fourth(q)
        return 0

    lax.fori_loop(1, 3, fourth_pair, 0)
    for i in (1, 2):
        send(cpart.at[i], rpart.at[0, THERE[i]], cy_s.at[i], cy_r.at[THERE[i]], ypeer(i))
    fourth(0)

    def join(values):
        peak = functools.reduce(jnp.maximum, values)
        return peak + jnp.log2(sum(jnp.exp2(v - peak) for v in values))

    values = [cpart[0]]
    for i in range(1, SIDE):
        remote(cpart.at[0], rpart.at[0, i], cy_s.at[i], cy_r.at[i], sibling).wait_recv()
        values.append(rpart[0, i])
    own = join(values)
    cpart[4] = own
    for o in range(1, ROWS):
        send(cpart.at[4], rpart.at[1, ROWS - o], rr_s.at[o], rr_r.at[ROWS - o], rpeer(o))
    values = [own]
    for o in range(1, ROWS):
        remote(cpart.at[4], rpart.at[1, o], rr_s.at[o], rr_r.at[o], sibling).wait_recv()
        values.append(rpart[1, o])
    gp_ref[...] = EPSILON * lb_ref[...] - (EPSILON * LN2) * (join(values) - g_ref[...] * KAPPA)
    for copy in sends:
        copy.wait_send()


def per_device(src_emb, tgt_emb, log_a, log_b, g_init, lists, counts):
    blocks = lists.shape[0]
    ids = jnp.where(jnp.arange(KC, dtype=jnp.int32)[None, :] < counts, lists.reshape(blocks, KC), NOSLOT)
    ids = jnp.pad(ids.reshape(SIDE, 1, SIDE * SBD * KC), ((0, 0), (0, 7), (0, 64)))
    la = jnp.pad(log_a.reshape(SBD, BC), ((0, 8 - SBD), (0, 0)))
    f32, bf16 = jnp.float32, jnp.bfloat16
    dma4 = pltpu.SemaphoreType.DMA((SIDE,))
    f, g = pl.pallas_call(
        kernel,
        out_shape=(jax.ShapeDtypeStruct((SBD, BC), f32), jax.ShapeDtypeStruct((TBC, BC), f32)),
        in_specs=[pl.BlockSpec(memory_space=pltpu.VMEM)] * 6,
        out_specs=(pl.BlockSpec(memory_space=pltpu.VMEM),) * 2,
        scratch_shapes=[
            pltpu.VMEM((SIDE, LAT, SBD * BC), f32),
            pltpu.VMEM((SIDE, LAT, TBC * BC), f32),
            pltpu.VMEM((SIDE, 8, BC), f32),
            pltpu.VMEM((SIDE, TBC, BC), f32),
            pltpu.VMEM((SIDE, 8, 128), jnp.int32),
            pltpu.SMEM((SIDE, 8, 128), jnp.int32),
            pltpu.VMEM((SIDE * SBD, BC, 256), bf16),
            pltpu.VMEM((SIDE * TBC + 1, 256, BC), bf16),
            pltpu.VMEM((SIDE * SBD, BC, 128), f32),
            pltpu.VMEM((SIDE * SBD, BC, 128), f32),
            pltpu.VMEM((STORED, BC, BC), f32),
            pltpu.VMEM((BC, 128), f32),
            pltpu.VMEM((SIDE, SIDE * SBD, BC), f32),
            pltpu.VMEM((SIDE, SBD, BC), f32),
            pltpu.VMEM((SIDE * SIDE, SBD * KC, BC), f32),
            pltpu.VMEM((SIDE * SIDE, SBD * KC, BC), f32),
            pltpu.VMEM((SIDE * SIDE, SBD * KC, BC), jnp.int32),
            pltpu.VMEM((SIDE + 1, TBC, BC), f32),
            pltpu.VMEM((2, ROWS, TBC, BC), f32),
        ] + [dma4] * 16 + [pltpu.SemaphoreType.DMA((ROWS,))] * 2 + [pltpu.SemaphoreType.DMA],
        compiler_params=pltpu.CompilerParams(
            collective_id=0, has_side_effects=True, vmem_limit_bytes=63 * 2**20),
        name="sinkhorn",
    )(src_emb, tgt_emb, la, g_init.reshape(TBC, BC), log_b.reshape(TBC, BC), ids)
    return f.reshape(-1), g.reshape(-1)


def solution(mesh):
    in_specs = (
        P(None, ("row", "col")),
        P(None, "col"),
        P(("row", "col")),
        P("col"),
        P("col"),
        P("row", "col", None),
        P("row", "col"),
    )
    return jax.shard_map(
        per_device, mesh=mesh, in_specs=in_specs, out_specs=(P(("row", "col")), P("col")), check_vma=False)
```

time: 499 us -> 77.7 us (0.16)
  matrix products: 155 us -> 0 us
  waiting for transfers between devices: 125 us -> 0 us
  other arithmetic: 77.2 us -> 0.67 us
  Pallas kernels: 0 us -> 68.9 us
  local copies, waits for them, and re-layouts: 70.2 us -> 7.04 us
  blocking collectives: 54.5 us -> 0 us
  between operations: 14 us -> 0.68 us
    dot_general x32 -> x0, matrix products: 155 us -> none  [pair_cost(): jnp.einsum('gli,gelj->geij', xb, yb, precision=lax.Precision.HIGHEST)]
    all_gather x3 -> x0, waiting for transfers between devices: 124 us -> none  [the longest x2 73.1 us: combined_all(): pieces = jax.tree.map(lambda part: lax.all_gather(part, axis), value)]
    pallas_call x0 -> x1, Pallas kernels: none -> 68.9 us  [per_device(): pl.pallas_call(kernel, out_shape=(jax.ShapeDtypeStruct((SBD, BC), f32), j...]
    reduce_sum x97 -> x0, other arithmetic: 59.6 us -> none  [the longest x16 28.1 us: row_stats(): total = jnp.sum(jnp.exp(score - top[:, None, :, None]), axis=(1, 3))]
    all_gather x3 -> x0, blocking collectives: 54.5 us -> none  [the longest x2 35.1 us: combined_all(): pieces = jax.tree.map(lambda part: lax.all_gather(part, axis), value)]
    gather x64 -> x0, local copies, waits for them, and re-layouts: 28 us -> none  [the longest x32 9.38 us: row_stats(): score = (gblocks[chosen][:, :, None, :] - cost) / EPSILON]
    dynamic_slice x16 -> x0, local copies, waits for them, and re-layouts: 17.7 us -> none  [the longest x15 17.1 us: combined_all(): lax.scan(lambda subtotal, piece: (join(subtotal, piece), None), head, tail)]
    select_n x32 -> x1, other arithmetic: 11 us -> 0.01 us  [per_device(): jnp.where(jnp.arange(KC, dtype=jnp.int32)[None, :] < counts, lists.reshap...]
  transfers between devices with their start and end apart: 3 -> 0, of which waited for: 3 -> 0; matrix products, arithmetic and copies ran while one was open for 2% -> 0% of each run, Pallas kernels for 0% -> 0%
where the time goes in v1:
time: 77.7 us; the launch traced here: 77.3 us
  Pallas kernels  68.9 us (89%)
  local copies, waits for them, and re-layouts  7.04 us (9%)
    pallas_call x1, Pallas kernels, per_device(): pl.pallas_call(kernel, out_shape=(jax.ShapeDtypeStruct((SBD, BC), f32), j...  68.9 us
    unnamed x16, local copies, waits for them, and re-layouts  4.2 us

profile of v1, /device:TPU:1, one launch (start us, length us, event | category | flops | bytes accessed | tf_op | source)
XLA Modules:
  0.0 77.3 jit_solution(1344847215121623699)
XLA Ops:
  0.6 0.0 copy-start.5
  0.6 0.5 broadcast.32
  1.2 0.1 copy-done.5
  1.3 0.7 reduce.3
  1.9 0.1 lt.31
  2.0 0.1 lt.32
  2.1 0.0 copy-start.4
  2.1 0.1 lt.33
  2.2 0.6 copy-done.4
  2.8 0.1 copy.11
  2.9 0.1 reshape.75
  3.0 0.1 lt.29
  3.1 0.0 copy-start.2
  3.1 0.6 pad.9.ids_ref
  3.7 0.1 copy-done.2
  3.8 0.0 copy-start
  3.8 0.6 pad.8.la_ref
  4.4 0.1 copy-done
  4.5 0.0 copy-start.1
  4.5 0.6 reshape.73.g_ref
  5.1 0.1 copy-done.1
  5.2 0.6 reshape.74.lb_ref
  5.8 68.9 %sinkhorn.1 = (f32[4,256]{1,0:T(4,128)}, f32[8,256]{1,0:T(8,128)}) custom-call(f32[32,1024]{1,0:T(8,128)} %x_ref.1, f32[32,2048]{1,0:T(8,128)} %y_ref.1, f32[8,256]{1,0:T(8,128)} %pad.8.la_ref, f32[8,256]{1,0:T(8,128)} %reshape.73.g_ref, f32[8,256]{1,0:T(8,128)} %reshape.74.lb_ref, s32[4,8,128]{2,1,0:T(8,128)} %pad.9.ids_ref), custom_call_target="tpu_custom_call" | custom-call | tf_op jit(solution)/shard_map/sinkhorn/pallas_call | solution.py:347
  74.7 1.3 %copy.14 = f32[1,2,8,128]{3,1,2,0:T(2,128)} copy(f32[1,2,8,128]{3,2,1,0:T(8,128)} %bitcast.12) | data formatting | bytes 16384
  76.0 0.0 copy-start.3
  76.0 0.7 copy-done.3
  76.7 0.6 copy.13
  (3 shorter events, 0.0 us)
Async XLA Ops:
  0.6 0.7 copy-start.5
  2.1 0.7 copy-start.4
  3.1 0.7 copy-start.2
  3.8 0.7 copy-start
  4.5 0.7 copy-start.1
  76.0 0.7 copy-start.3

commit v2 on v1

v2 whole, which is shorter than its diff:
```python
import functools

import jax
import jax.numpy as jnp
from jax import lax
from jax.experimental import pallas as pl
from jax.experimental.pallas import tpu as pltpu
from jax.sharding import PartitionSpec as P

MESH = pl.DeviceIdType.MESH
LAT = 32
BC = 256
TBC = 8
KC = 4
SIDE = 4
ROWS = 16
SBD = 4
NOSLOT = 8
NEG = -1e30
EPSILON = 2.0
LOG2E = 1.4426950408889634
LN2 = 0.6931471805599453
KAPPA = LOG2E / EPSILON
OFFSETS = (0, 1, 3, 2)
THERE = (0, 2, 1, 3)
STORED = 3 * SIDE * KC


def split3(v):
    hi = v.astype(jnp.bfloat16)
    rest = v - hi.astype(jnp.float32)
    mid = rest.astype(jnp.bfloat16)
    low = (rest - mid.astype(jnp.float32)).astype(jnp.bfloat16)
    return hi, mid, low


def bias_rows(first, second):
    row = lax.broadcasted_iota(jnp.int32, (LAT, BC), 0)
    out = jnp.zeros((LAT, BC), jnp.float32)
    for k, v in enumerate(tuple(first) + tuple(second)):
        v = 1.0 if v is None else v.astype(jnp.float32)
        out = jnp.where(row == k, v, out)
    return out.astype(jnp.bfloat16)


def gray(i):
    return i + i // 2 - 2 * (i // 3)


def kernel(
    x_ref, y_ref, la_ref, g_ref, lists_ref, counts_ref, f_ref, gp_ref,
    xg, yg, lag, gg, idg, ids, lhs, rhs, m0, m1, m2, m3, s0, s1, s2, s3, k0, k1, k2, k3, part, uall, cm, cs, idv, cpart, rpart,
    xs_s, xs_r, ys_s, ys_r, yf_s, yf_r, la_s, la_r, g_s, g_r, id_s, id_r, cy_s, cy_r, ex_s, ex_r, rr_s, rr_r, loc,
):
    mrow, srow, keep = (m0, m1, m2, m3), (s0, s1, s2, s3), (k0, k1, k2, k3)
    row = lax.axis_index("row")
    col = lax.axis_index("col")
    yme, xme = col // SIDE, col % SIDE
    core = row % 2
    half = LAT // 2
    sibling = (row + 1 - 2 * core, col)

    def xpeer(i):
        return (row, yme * SIDE + (xme + OFFSETS[i]) % SIDE)

    def ypeer(i):
        return (row, ((yme + OFFSETS[i]) % SIDE) * SIDE + xme)

    def zpeer(d):
        return ((row + 2 * d) % ROWS, col)

    barrier = pltpu.get_barrier_semaphore()
    for i in range(1, SIDE):
        pl.semaphore_signal(barrier, inc=1, device_id=xpeer(i), device_id_type=MESH)
        pl.semaphore_signal(barrier, inc=1, device_id=ypeer(i), device_id_type=MESH)
    for d in range(1, ROWS // 2):
        pl.semaphore_signal(barrier, inc=1, device_id=zpeer(d), device_id_type=MESH)
    pl.semaphore_signal(barrier, inc=1, device_id=sibling, device_id_type=MESH)

    xg[0] = x_ref[...]
    yg[0] = y_ref[...]
    lag[xme] = la_ref[...]
    gg[0] = g_ref[...]
    slot = lax.broadcasted_iota(jnp.int32, (KC, ROWS * SBD), 0)
    idg[0] = jnp.full((8, 128), NOSLOT, jnp.int32)
    idg[0, :KC, :ROWS * SBD] = jnp.where(slot < counts_ref[...], lists_ref[...], NOSLOT)

    rhs[SIDE * TBC] = jnp.concatenate(
        [jnp.zeros((96, BC), jnp.bfloat16)]
        + [bias_rows([None] * 3, [jnp.full((1, BC), NEG, jnp.float32)] + [jnp.zeros((1, BC), jnp.float32)] * 2)]
        + [jnp.zeros((128, BC), jnp.bfloat16)], axis=0)

    def init(xi, _):
        for b in range(SBD):
            mrow[b][xi] = jnp.full((BC, 128), NEG, jnp.float32)
            srow[b][xi] = jnp.zeros((BC, 128), jnp.float32)
        return 0

    lax.fori_loop(0, SIDE, init, 0)

    pl.semaphore_wait(barrier, 2 * (SIDE - 1) + ROWS // 2)

    def remote(src, dst, s, r, dev):
        return pltpu.make_async_remote_copy(
            src_ref=src, dst_ref=dst, send_sem=s, recv_sem=r, device_id=dev, device_id_type=MESH)

    mine = pl.ds(pl.multiple_of(core * half, half), half)
    theirs = pl.ds(pl.multiple_of((1 - core) * half, half), half)

    def sends(i):
        t = THERE[i]
        return [
            remote(x_ref, xg.at[t], xs_s.at[t], xs_r.at[t], xpeer(i)),
            remote(y_ref.at[mine], yg.at[t, mine], ys_s.at[t], ys_r.at[t], ypeer(i)),
            remote(idg.at[0], idg.at[t], id_s.at[t], id_r.at[t], ypeer(i)),
            remote(g_ref, gg.at[t], g_s.at[t], g_r.at[t], ypeer(i)),
            remote(la_ref, lag.at[xme], la_s.at[t], la_r.at[t], xpeer(i)),
        ]

    def row_send(i, a):
        return remote(part.at[0, a], part.at[THERE[i], a], ex_s.at[i, a], ex_r.at[THERE[i], a], xpeer(i))

    def col_send(i):
        return remote(cpart.at[i], rpart.at[0, THERE[i]], cy_s.at[i], cy_r.at[THERE[i]], ypeer(i))

    def pair_send():
        return remote(cpart.at[SIDE], rpart.at[1, 0], rr_s.at[0], rr_r.at[0], sibling)

    def last_send(d):
        return remote(cpart.at[SIDE + 1], rpart.at[1, ROWS // 2 - d], rr_s.at[d], rr_r.at[ROWS // 2 - d], zpeer(d))

    for i in (1, 2):
        for copy in sends(i):
            copy.start()

    def await_x(i):
        remote(x_ref, xg.at[i], xs_s.at[i], xs_r.at[i], sibling).wait_recv()

    def forward_y(i):
        remote(y_ref.at[mine], yg.at[i, mine], ys_s.at[i], ys_r.at[i], sibling).wait_recv()
        remote(yg.at[i, mine], yg.at[i, mine], yf_s.at[i], yf_r.at[i], sibling).start()

    def await_y(i):
        remote(yg.at[i, mine], yg.at[i, theirs], yf_s.at[i], yf_r.at[i], sibling).wait()
        remote(g_ref, gg.at[i], g_s.at[i], g_r.at[i], sibling).wait_recv()
        remote(idg.at[0], idg.at[i], id_s.at[i], id_r.at[i], sibling).wait_recv()

    def prep_x(i):
        def one(b, _):
            v = xg[i, :, pl.ds(pl.multiple_of(b * BC, BC), BC)]
            hi, mid, low = split3(v * KAPPA)
            norm = jnp.sum(v * v, axis=0, keepdims=True) * (-0.5 * KAPPA)
            z = jnp.concatenate(
                [hi, mid, low, bias_rows(split3(norm), [None] * 3), hi, mid, hi, jnp.zeros((LAT, BC), jnp.bfloat16)], axis=0)
            lhs[i * SBD + b] = z.T
            return 0

        lax.fori_loop(0, SBD, one, 0)

    def prep_y(i):
        def one(t, _):
            v = yg[i, :, pl.ds(pl.multiple_of(t * BC, BC), BC)]
            hi, mid, low = split3(v)
            bias = jnp.concatenate([gg[i, pl.ds(2 * t, 1), :], gg[i, pl.ds(2 * t + 1, 1), :]], axis=1) * KAPPA - jnp.sum(v * v, axis=0, keepdims=True) * (0.5 * KAPPA)
            rhs[i * TBC + t] = jnp.concatenate(
                [hi, hi, hi, bias_rows([None] * 3, split3(bias)), mid, mid, low, jnp.zeros((LAT, BC), jnp.bfloat16)], axis=0)
            return 0

        lax.fori_loop(0, TBC, one, 0)
        copy = pltpu.make_async_copy(idg.at[i], ids.at[i], loc)
        copy.start()
        copy.wait()

    def listed(xi, yi, b, k):
        return ids[yi, k, (yme * SIDE + (xme + gray(xi)) % SIDE) * SBD + b]

    def score(xi, yi, b, k):
        t = listed(xi, yi, b, k)
        t = jnp.where(t == NOSLOT, SIDE * TBC, yi * TBC + t)
        return jnp.dot(lhs[xi * SBD + b], rhs[t], preferred_element_type=jnp.float32)

    def row_step(xi, yi, kept):
        tops, tiles = {}, {}

        def scores(b):
            top = mrow[b][xi]
            for k in range(KC):
                v = score(xi, yi, b, k)
                if kept:
                    keep[b][(yi * SIDE + xi) * KC + k] = v
                    v = keep[b].at[(yi * SIDE + xi) * KC + k]
                top = jnp.maximum(top, jnp.maximum(v[:, :128], v[:, 128:]))
                tiles[b, k] = v
            tops[b] = top

        def sums(b):
            top = tops[b]
            total = srow[b][xi] * jnp.exp2(mrow[b][xi] - top)
            for k in range(KC):
                v = tiles[b, k]
                total = total + (jnp.exp2(v[:, :128] - top) + jnp.exp2(v[:, 128:] - top))
            mrow[b][xi] = top
            srow[b][xi] = total

        for b in range(SBD):
            scores(b)
            sums(b)

    def first(s, _):
        early = s < 9
        xi = jnp.where(early, s % 3, SIDE - 1)
        yi = jnp.where(early, s // 3, s - 9)

        @pl.when((s == 1) | (s == 2) | (s == 9))
        def _():
            await_x(xi)

        @pl.when(s == 1)
        def _():
            for copy in sends(3):
                copy.start()
            forward_y(1)
            forward_y(2)

        @pl.when(s == 9)
        def _():
            forward_y(3)

        @pl.when((s == 3) | (s == 6))
        def _():
            await_y(yi)

        @pl.when((s < 3) | (s == 9))
        def _():
            prep_x(xi)

        @pl.when((s == 0) | (s == 3) | (s == 6))
        def _():
            prep_y(yi)

        row_step(xi, yi, True)
        return 0

    lax.fori_loop(0, 12, first, 0)
    await_y(3)
    prep_y(3)

    lane = lax.broadcasted_iota(jnp.int32, (BC, 128), 1)

    def second(a, _):
        xi = gray((a - xme + SIDE) % SIDE)
        row_step(xi, SIDE - 1, False)
        out = jnp.zeros((BC, 128), jnp.float32)
        for b in range(SBD):
            m = mrow[b][xi]
            top = jnp.max(m, axis=1, keepdims=True)
            total = jnp.sum(srow[b][xi] * jnp.exp2(m - top), axis=1, keepdims=True)
            out = jnp.where(lane == b, top + jnp.log2(total), out)
        part[0, a] = out.T[:8]
        for i in range(1, SIDE):
            row_send(i, a).start()
        return 0

    lax.fori_loop(0, SIDE, second, 0)
    for i in range(1, SIDE):
        remote(la_ref, lag.at[0], la_s.at[i], la_r.at[i], sibling).wait_recv()

    def potential(a):
        xi = gray((a - xme + SIDE) % SIDE)
        parts = [part[0, a]]
        for i in range(1, SIDE):
            remote(part.at[0, a], part.at[i, a], ex_s.at[i, a], ex_r.at[i, a], sibling).wait_recv()
            parts.append(part[i, a])
        top = functools.reduce(jnp.maximum, parts)
        lse = top + jnp.log2(sum(jnp.exp2(v - top) for v in parts))
        mass = jnp.concatenate(
            [jnp.concatenate([lag[a, 2 * b:2 * b + 1], lag[a, 2 * b + 1:2 * b + 2]], axis=1) for b in range(SBD)]
            + [jnp.zeros((8 - SBD, BC), jnp.float32)], axis=0)
        u = mass * LOG2E - lse
        for b in range(SBD):
            for h in range(2):
                uall[a, 2 * b + h:2 * b + h + 1, :] = u[b:b + 1, h * 128:(h + 1) * 128]
        across = jnp.concatenate([u, jnp.zeros((120, BC), jnp.float32)], axis=0).T
        for b in range(SBD):
            mrow[b][xi] = jnp.broadcast_to(across[:, b:b + 1], (BC, 128))
        return xi

    def col_step(xi, yi, kept):
        for b in range(SBD):
            for k in range(KC):
                if kept:
                    v = keep[b].at[(yi * SIDE + xi) * KC + k]
                else:
                    v = score(xi, yi, b, k)
                at = b * KC + k
                for h in range(2):
                    lanes = slice(h * 128, (h + 1) * 128)
                    t = (v[:, lanes] + mrow[b][xi]).reshape(BC // 8, 8, 128)
                    peak = jnp.max(jnp.max(t, axis=0), axis=0, keepdims=True)
                    total = jnp.sum(jnp.sum(jnp.exp2(t - peak), axis=0), axis=0, keepdims=True)
                    cm[yi * SIDE + xi, at:at + 1, lanes] = peak
                    cs[yi * SIDE + xi, at:at + 1, lanes] = total
                idv[yi * SIDE + xi, at:at + 1, :] = jnp.full((1, BC), listed(xi, yi, b, k), jnp.int32)

    def finish_cols(yi):
        group = pl.ds(yi * SIDE, SIDE)
        for t in range(TBC):
            hit = idv[group] == t
            m = cm[group]
            peak = jnp.max(jnp.where(hit, m, NEG).reshape(-1, BC), axis=0, keepdims=True)
            total = jnp.where(hit, cs[group] * jnp.exp2(m - peak[None]), 0.0)
            total = jnp.sum(total.reshape(-1, BC), axis=0, keepdims=True)
            some = total > 0.0
            value = jnp.where(some, peak + jnp.log2(jnp.where(some, total, 1.0)), NEG)
            for h in range(2):
                cpart[yi, 2 * t + h:2 * t + h + 1, :] = value[:, h * 128:(h + 1) * 128]

    def third(a, _):
        col_step(potential(a), SIDE - 1, False)
        return 0

    lax.fori_loop(0, SIDE, third, 0)
    f_ref[...] = uall[xme]
    finish_cols(SIDE - 1)
    col_send(3).start()

    def fourth(yi):
        def body(xi, _):
            col_step(xi, yi, True)
            return 0

        lax.fori_loop(0, SIDE, body, 0)
        finish_cols(yi)

    def fourth_pair(q, _):
        fourth(q)
        return 0

    lax.fori_loop(1, 3, fourth_pair, 0)
    for i in (1, 2):
        col_send(i).start()
    fourth(0)

    def join(values):
        peak = functools.reduce(jnp.maximum, values)
        return peak + jnp.log2(sum(jnp.exp2(v - peak) for v in values))

    values = [cpart[0]]
    for i in range(1, SIDE):
        remote(cpart.at[0], rpart.at[0, i], cy_s.at[i], cy_r.at[i], sibling).wait_recv()
        values.append(rpart[0, i])
    cpart[SIDE] = join(values)
    pair_send().start()
    remote(cpart.at[SIDE], rpart.at[1, 0], rr_s.at[0], rr_r.at[0], sibling).wait_recv()
    both = join([cpart[SIDE], rpart[1, 0]])
    cpart[SIDE + 1] = both
    for d in range(1, ROWS // 2):
        last_send(d).start()
    values = [both]
    for d in range(1, ROWS // 2):
        remote(cpart.at[SIDE], rpart.at[1, d], rr_s.at[d], rr_r.at[d], sibling).wait_recv()
        values.append(rpart[1, d])
    gp_ref[...] = join(values)
    for i in range(1, SIDE):
        for copy in sends(i) + [col_send(i)] + [row_send(i, a) for a in range(SIDE)]:
            copy.wait_send()
    pair_send().wait_send()
    for d in range(1, ROWS // 2):
        last_send(d).wait_send()


def per_device(src_emb, tgt_emb, log_a, log_b, g_init, lists, counts):
    f32, bf16 = jnp.float32, jnp.bfloat16
    dma4 = pltpu.SemaphoreType.DMA((SIDE,))
    u, lse = pl.pallas_call(
        kernel,
        out_shape=(jax.ShapeDtypeStruct((8, 128), f32), jax.ShapeDtypeStruct((16, 128), f32)),
        in_specs=[pl.BlockSpec(memory_space=pltpu.VMEM)] * 6,
        out_specs=(pl.BlockSpec(memory_space=pltpu.VMEM),) * 2,
        scratch_shapes=[
            pltpu.VMEM((SIDE, LAT, SBD * BC), f32),
            pltpu.VMEM((SIDE, LAT, TBC * BC), f32),
            pltpu.VMEM((SIDE, 8, 128), f32),
            pltpu.VMEM((SIDE, 16, 128), f32),
            pltpu.VMEM((SIDE, 8, 128), jnp.int32),
            pltpu.SMEM((SIDE, 8, 128), jnp.int32),
            pltpu.VMEM((SIDE * SBD, BC, 256), bf16),
            pltpu.VMEM((SIDE * TBC + 1, 256, BC), bf16),
        ] + [pltpu.VMEM((SIDE, BC, 128), f32)] * (2 * SBD) + [pltpu.VMEM((STORED, BC, BC), f32)] * SBD + [
            pltpu.VMEM((SIDE, SIDE, 8, BC), f32),
            pltpu.VMEM((SIDE, 8, 128), f32),
            pltpu.VMEM((SIDE * SIDE, SBD * KC, BC), f32),
            pltpu.VMEM((SIDE * SIDE, SBD * KC, BC), f32),
            pltpu.VMEM((SIDE * SIDE, SBD * KC, BC), jnp.int32),
            pltpu.VMEM((SIDE + 2, 16, 128), f32),
            pltpu.VMEM((2, ROWS, 16, 128), f32),
        ] + [dma4] * 14 + [pltpu.SemaphoreType.DMA((SIDE, SIDE))] * 2 + [pltpu.SemaphoreType.DMA((ROWS // 2,))] * 2 + [pltpu.SemaphoreType.DMA],
        compiler_params=pltpu.CompilerParams(
            collective_id=0, has_side_effects=True, vmem_limit_bytes=63 * 2**20),
        name="sinkhorn",
    )(src_emb, tgt_emb, log_a.reshape(8, 128), g_init.reshape(16, 128),
      lists.transpose(1, 2, 0).reshape(KC, ROWS * SBD), counts.reshape(1, ROWS * SBD))
    f = u.reshape(-1) * (EPSILON * LN2)
    g = EPSILON * log_b - (EPSILON * LN2) * (lse.reshape(-1) - g_init * KAPPA)
    return f, g


def solution(mesh):
    in_specs = (
        P(None, ("row", "col")),
        P(None, "col"),
        P(("row", "col")),
        P("col"),
        P("col"),
        P("row", "col", None),
        P("row", "col"),
    )
    return jax.shard_map(
        per_device, mesh=mesh, in_specs=in_specs, out_specs=(P(("row", "col")), P("col")), check_vma=False)
```

time: 77.7 us -> 63.5 us (0.82)
  Pallas kernels: 68.9 us -> 60.1 us
  local copies, waits for them, and re-layouts: 7.04 us -> 0.01 us
  other arithmetic: 0.67 us -> 2.57 us
    pallas_call x1, Pallas kernels: 68.9 us -> 60.1 us  [per_device(): pl.pallas_call(kernel, out_shape=(jax.ShapeDtypeStruct((8, 128), f32), ja...]
    unnamed x16 -> x4, local copies, waits for them, and re-layouts: 4.2 us -> 0.01 us
    sub x0 -> x1, other arithmetic: none -> 1.3 us  [per_device(): g = EPSILON * log_b - EPSILON * LN2 * (lse.reshape(-1) - g_init * KAPPA)]
    reshape x4 -> x0, local copies, waits for them, and re-layouts: 1.3 us -> none  [the longest x1 0.6 us: per_device(): log_b.reshape(TBC, BC)]
    mul x0 -> x1, other arithmetic: none -> 1.27 us  [per_device(): f = u.reshape(-1) * (EPSILON * LN2)]
    pad x2 -> x0, local copies, waits for them, and re-layouts: 1.21 us -> none  [the longest x1 0.6 us: per_device(): jnp.pad(ids.reshape(SIDE, 1, SIDE * SBD * KC), ((0, 0), (0, 7), (0, 64)))]
where the time goes in v2:
time: 63.5 us; the launch traced here: 63.3 us
  Pallas kernels  60.1 us (95%)
  other arithmetic  2.57 us (4%)
  between operations  0.66 us (1%)
    pallas_call x1, Pallas kernels, per_device(): pl.pallas_call(kernel, out_shape=(jax.ShapeDtypeStruct((8, 128), f32), ja...  60.1 us
    sub x1, other arithmetic, per_device(): g = EPSILON * log_b - EPSILON * LN2 * (lse.reshape(-1) - g_init * KAPPA)  1.3 us
    mul x1, other arithmetic, per_device(): f = u.reshape(-1) * (EPSILON * LN2)  1.27 us

profile of v2, /device:TPU:1, one launch (start us, length us, event | category | flops | bytes accessed | tf_op | source)
XLA Modules:
  0.0 63.3 jit_solution(144984546942608810)
XLA Ops:
  0.6 0.0 copy-start.1
  0.6 60.1 %sinkhorn.1 = (f32[8,128]{1,0:T(8,128)}, f32[16,128]{1,0:T(8,128)}) custom-call(f32[32,1024]{1,0:T(8,128)} %x_ref.1, f32[32,2048]{1,0:T(8,128)} %y_ref.1, f32[8,128]{1,0:T(8,128)} %bitcast.15, f32[16,128]{1,0:T(8,128)} %bitcast.14, s32[4,64]{1,0:T(4,128)} %bitcast.16, s32[1,64]{1,0:T(1,128)} %bitcast.17), custom_call_target="tpu_custom_call" | custom-call | tf_op jit(solution)/shard_map/sinkhorn/pallas_call | solution.py:375
  60.7 0.0 copy-start
  60.8 1.3 %multiply_bitcast_fusion = f32[1024]{0:T(1024)} fusion(f32[8,128]{1,0:T(8,128)} %get-tuple-element.4), kind=kLoop, calls=%fused_computation.3 | loop fusion | flops 1024 | bytes 8192 | tf_op jit(solution)/shard_map/mul | solution.py:403
  62.0 0.0 copy-done.1
  62.0 0.0 copy-done
  62.0 1.3 %fusion.1 = f32[2048]{0:T(1024)} fusion(f32[16,128]{1,0:T(8,128)} %get-tuple-element.5, f32[2048]{0:T(1024)S(1)} %copy-done, f32[2048]{0:T(1024)S(1)} %copy-done.1), kind=kLoop, calls=%fused_computation.2 | loop fusion | flops 10240 | bytes 32768 | tf_op jit(solution)/shard_map/sub | solution.py:404
Async XLA Ops:
  0.6 61.4 %copy-start.1 = (f32[2048]{0:T(1024)S(1)}, f32[2048]{0:T(1024)}, u32[]{:S(2)}) copy-start(f32[2048]{0:T(1024)} %param.10) | copy-start | bytes 24580
  60.7 1.3 %copy-start = (f32[2048]{0:T(1024)S(1)}, f32[2048]{0:T(1024)}, u32[]{:S(2)}) copy-start(f32[2048]{0:T(1024)} %param.11) | copy-start | bytes 24580

commit v3 on v2

--- a/solution.py
+++ b/solution.py
@@ -287,33 +287,48 @@
 
     def col_step(xi, yi, kept):
         for b in range(SBD):
+            vs = []
             for k in range(KC):
-                if kept:
-                    v = keep[b].at[(yi * SIDE + xi) * KC + k]
-                else:
-                    v = score(xi, yi, b, k)
-                at = b * KC + k
-                for h in range(2):
-                    lanes = slice(h * 128, (h + 1) * 128)
-                    t = (v[:, lanes] + mrow[b][xi]).reshape(BC // 8, 8, 128)
-                    peak = jnp.max(jnp.max(t, axis=0), axis=0, keepdims=True)
-                    total = jnp.sum(jnp.sum(jnp.exp2(t - peak), axis=0), axis=0, keepdims=True)
+                vs.append(keep[b].at[(yi * SIDE + xi) * KC + k] if kept else score(xi, yi, b, k))
+                idv[yi * SIDE + xi, b * KC + k:b * KC + k + 1, :] = jnp.full((1, BC), listed(xi, yi, b, k), jnp.int32)
+            for h in range(2):
+                lanes = slice(h * 128, (h + 1) * 128)
+                ps = [[] for _ in range(KC)]
+                ts = [[] for _ in range(KC)]
+                for r in range(0, BC, 64):
+                    rows = slice(r, r + 64)
+                    u = mrow[b][xi, rows]
+                    for k in range(KC):
+                        t = (vs[k][rows, lanes] + u).reshape(64 // 8, 8, 128)
+                        p = jnp.max(t, axis=0)
+                        ps[k].append(p)
+                        ts[k].append(jnp.sum(jnp.exp2(t - p), axis=0))
+                for k in range(KC):
+                    at = b * KC + k
+                    m8 = functools.reduce(jnp.maximum, ps[k])
+                    peak = jnp.max(m8, axis=0, keepdims=True)
+                    total = sum(q * jnp.exp2(p - peak) for q, p in zip(ts[k], ps[k]))
                     cm[yi * SIDE + xi, at:at + 1, lanes] = peak
-                    cs[yi * SIDE + xi, at:at + 1, lanes] = total
-                idv[yi * SIDE + xi, at:at + 1, :] = jnp.full((1, BC), listed(xi, yi, b, k), jnp.int32)
+                    cs[yi * SIDE + xi, at:at + 1, lanes] = jnp.sum(total, axis=0, keepdims=True)
 
     def finish_cols(yi):
         group = pl.ds(yi * SIDE, SIDE)
+        ids_v = idv[group].reshape(-1, BC)
+        m = cm[group].reshape(-1, BC)
+        c = cs[group].reshape(-1, BC)
+        peaks, totals = [], []
         for t in range(TBC):
-            hit = idv[group] == t
-            m = cm[group]
-            peak = jnp.max(jnp.where(hit, m, NEG).reshape(-1, BC), axis=0, keepdims=True)
-            total = jnp.where(hit, cs[group] * jnp.exp2(m - peak[None]), 0.0)
-            total = jnp.sum(total.reshape(-1, BC), axis=0, keepdims=True)
-            some = total > 0.0
-            value = jnp.where(some, peak + jnp.log2(jnp.where(some, total, 1.0)), NEG)
+            hit = ids_v == t
+            peak = jnp.max(jnp.where(hit, m, NEG), axis=0, keepdims=True)
+            peaks.append(peak)
+            totals.append(jnp.sum(jnp.where(hit, c * jnp.exp2(m - peak), 0.0), axis=0, keepdims=True))
+        peak = jnp.concatenate(peaks, axis=0)
+        total = jnp.concatenate(totals, axis=0)
+        some = total > 0.0
+        value = jnp.where(some, peak + jnp.log2(jnp.where(some, total, 1.0)), NEG)
+        for t in range(TBC):
             for h in range(2):
-                cpart[yi, 2 * t + h:2 * t + h + 1, :] = value[:, h * 128:(h + 1) * 128]
+                cpart[yi, 2 * t + h:2 * t + h + 1, :] = value[t:t + 1, h * 128:(h + 1) * 128]
 
     def third(a, _):
         col_step(potential(a), SIDE - 1, False)
@@ -367,6 +382,11 @@
     pair_send().wait_send()
     for d in range(1, ROWS // 2):
         last_send(d).wait_send()
+
+
+def finish(u_ref, lse_ref, g_ref, lb_ref, f_ref, gp_ref):
+    f_ref[...] = u_ref[...] * (EPSILON * LN2)
+    gp_ref[...] = EPSILON * lb_ref[...] - (EPSILON * LN2) * (lse_ref[...] - g_ref[...] * KAPPA)
 
 
 def per_device(src_emb, tgt_emb, log_a, log_b, g_init, lists, counts):
@@ -400,9 +420,14 @@
         name="sinkhorn",
     )(src_emb, tgt_emb, log_a.reshape(8, 128), g_init.reshape(16, 128),
       lists.transpose(1, 2, 0).reshape(KC, ROWS * SBD), counts.reshape(1, ROWS * SBD))
-    f = u.reshape(-1) * (EPSILON * LN2)
-    g = EPSILON * log_b - (EPSILON * LN2) * (lse.reshape(-1) - g_init * KAPPA)
-    return f, g
+    f, g = pl.pallas_call(
+        finish,
+        out_shape=(jax.ShapeDtypeStruct((8, 128), f32), jax.ShapeDtypeStruct((16, 128), f32)),
+        in_specs=[pl.BlockSpec(memory_space=pltpu.VMEM)] * 4,
+        out_specs=(pl.BlockSpec(memory_space=pltpu.VMEM),) * 2,
+        name="finish",
+    )(u, lse, g_init.reshape(16, 128), log_b.reshape(16, 128))
+    return f.reshape(-1), g.reshape(-1)
 
 
 def solution(mesh):

time: 63.5 us -> 61.8 us (0.973)
  other arithmetic: 2.57 us -> 0 us
  Pallas kernels: 60.1 us -> 61 us
    pallas_call x0 -> x1, Pallas kernels: none -> 1.34 us  [per_device(): pl.pallas_call(finish, out_shape=(jax.ShapeDtypeStruct((8, 128), f32), ja...]
    sub x1 -> x0, other arithmetic: 1.3 us -> none  [per_device(): g = EPSILON * log_b - EPSILON * LN2 * (lse.reshape(-1) - g_init * KAPPA)]
    mul x1 -> x0, other arithmetic: 1.27 us -> none  [per_device(): f = u.reshape(-1) * (EPSILON * LN2)]
where the time goes in v3:
time: 61.8 us; the launch traced here: 61.6 us
  Pallas kernels  61 us (99%)
  between operations  0.64 us (1%)
    pallas_call x1, Pallas kernels, per_device(): pl.pallas_call(kernel, out_shape=(jax.ShapeDtypeStruct((8, 128), f32), ja...  59.7 us
    pallas_call x1, Pallas kernels, per_device(): pl.pallas_call(finish, out_shape=(jax.ShapeDtypeStruct((8, 128), f32), ja...  1.34 us

profile of v3, /device:TPU:1, one launch (start us, length us, event | category | flops | bytes accessed | tf_op | source)
XLA Modules:
  0.0 61.6 jit_solution(13657948858169170731)
XLA Ops:
  0.6 59.7 %sinkhorn.1 = (f32[8,128]{1,0:T(8,128)}, f32[16,128]{1,0:T(8,128)}) custom-call(f32[32,1024]{1,0:T(8,128)} %x_ref.1, f32[32,2048]{1,0:T(8,128)} %y_ref.1, f32[8,128]{1,0:T(8,128)} %bitcast.12, f32[16,128]{1,0:T(8,128)} %bitcast.9, s32[4,64]{1,0:T(4,128)} %bitcast.13, s32[1,64]{1,0:T(1,128)} %bitcast.14), custom_call_target="tpu_custom_call" | custom-call | tf_op jit(solution)/shard_map/sinkhorn/pallas_call | solution.py:395
  60.3 1.3 %finish.1 = (f32[8,128]{1,0:T(8,128)}, f32[16,128]{1,0:T(8,128)}) custom-call(f32[8,128]{1,0:T(8,128)} %get-tuple-element.6.u_ref, f32[16,128]{1,0:T(8,128)} %get-tuple-element.7.lse_ref, f32[16,128]{1,0:T(8,128)} %bitcast.10, f32[16,128]{1,0:T(8,128)} %bitcast.11), custom_call_target="tpu_custom_call" | custom-call | tf_op jit(solution)/shard_map/finish/pallas_call | solution.py:423

commit v4 on v3

--- a/solution.py
+++ b/solution.py
@@ -50,7 +50,7 @@
 def kernel(
     x_ref, y_ref, la_ref, g_ref, lists_ref, counts_ref, f_ref, gp_ref,
     xg, yg, lag, gg, idg, ids, lhs, rhs, m0, m1, m2, m3, s0, s1, s2, s3, k0, k1, k2, k3, part, uall, cm, cs, idv, cpart, rpart,
-    xs_s, xs_r, ys_s, ys_r, yf_s, yf_r, la_s, la_r, g_s, g_r, id_s, id_r, cy_s, cy_r, ex_s, ex_r, rr_s, rr_r, loc,
+    xs_s, xs_r, ys_s, ys_r, yf_s, yf_r, la_s, la_r, g_s, g_r, id_s, id_r, cy_s, cy_r, ex_s, ex_r, rr_s, rr_r, loc, in_sem, lists, counts,
 ):
     mrow, srow, keep = (m0, m1, m2, m3), (s0, s1, s2, s3), (k0, k1, k2, k3)
     row = lax.axis_index("row")
@@ -77,14 +77,14 @@
         pl.semaphore_signal(barrier, inc=1, device_id=zpeer(d), device_id_type=MESH)
     pl.semaphore_signal(barrier, inc=1, device_id=sibling, device_id_type=MESH)
 
-    xg[0] = x_ref[...]
-    yg[0] = y_ref[...]
-    lag[xme] = la_ref[...]
-    gg[0] = g_ref[...]
-    slot = lax.broadcasted_iota(jnp.int32, (KC, ROWS * SBD), 0)
-    idg[0] = jnp.full((8, 128), NOSLOT, jnp.int32)
-    idg[0, :KC, :ROWS * SBD] = jnp.where(slot < counts_ref[...], lists_ref[...], NOSLOT)
-
+    loads = [
+        pltpu.make_async_copy(a, b, in_sem.at[n])
+        for n, (a, b) in enumerate((
+            (x_ref, xg.at[0]), (y_ref, yg.at[0]), (la_ref, lag.at[xme]), (g_ref, gg.at[0]),
+            (lists_ref, lists), (counts_ref, counts)))
+    ]
+    for copy in loads:
+        copy.start()
     rhs[SIDE * TBC] = jnp.concatenate(
         [jnp.zeros((96, BC), jnp.bfloat16)]
         + [bias_rows([None] * 3, [jnp.full((1, BC), NEG, jnp.float32)] + [jnp.zeros((1, BC), jnp.float32)] * 2)]
@@ -98,6 +98,12 @@
 
     lax.fori_loop(0, SIDE, init, 0)
 
+    for copy in loads:
+        copy.wait()
+    slot = lax.broadcasted_iota(jnp.int32, (KC, ROWS * SBD), 0)
+    idg[0] = jnp.full((8, 128), NOSLOT, jnp.int32)
+    idg[0, :KC, :ROWS * SBD] = jnp.where(slot < counts[...], lists[...], NOSLOT)
+
     pl.semaphore_wait(barrier, 2 * (SIDE - 1) + ROWS // 2)
 
     def remote(src, dst, s, r, dev):
@@ -110,11 +116,11 @@
     def sends(i):
         t = THERE[i]
         return [
-            remote(x_ref, xg.at[t], xs_s.at[t], xs_r.at[t], xpeer(i)),
-            remote(y_ref.at[mine], yg.at[t, mine], ys_s.at[t], ys_r.at[t], ypeer(i)),
+            remote(xg.at[0], xg.at[t], xs_s.at[t], xs_r.at[t], xpeer(i)),
+            remote(yg.at[0, mine], yg.at[t, mine], ys_s.at[t], ys_r.at[t], ypeer(i)),
             remote(idg.at[0], idg.at[t], id_s.at[t], id_r.at[t], ypeer(i)),
-            remote(g_ref, gg.at[t], g_s.at[t], g_r.at[t], ypeer(i)),
-            remote(la_ref, lag.at[xme], la_s.at[t], la_r.at[t], xpeer(i)),
+            remote(gg.at[0], gg.at[t], g_s.at[t], g_r.at[t], ypeer(i)),
+            remote(lag.at[xme], lag.at[xme], la_s.at[t], la_r.at[t], xpeer(i)),
         ]
 
     def row_send(i, a):
@@ -134,15 +140,15 @@
             copy.start()
 
     def await_x(i):
-        remote(x_ref, xg.at[i], xs_s.at[i], xs_r.at[i], sibling).wait_recv()
+        remote(xg.at[0], xg.at[i], xs_s.at[i], xs_r.at[i], sibling).wait_recv()
 
     def forward_y(i):
-        remote(y_ref.at[mine], yg.at[i, mine], ys_s.at[i], ys_r.at[i], sibling).wait_recv()
+        remote(yg.at[0, mine], yg.at[i, mine], ys_s.at[i], ys_r.at[i], sibling).wait_recv()
         remote(yg.at[i, mine], yg.at[i, mine], yf_s.at[i], yf_r.at[i], sibling).start()
 
     def await_y(i):
         remote(yg.at[i, mine], yg.at[i, theirs], yf_s.at[i], yf_r.at[i], sibling).wait()
-        remote(g_ref, gg.at[i], g_s.at[i], g_r.at[i], sibling).wait_recv()
+        remote(gg.at[0], gg.at[i], g_s.at[i], g_r.at[i], sibling).wait_recv()
         remote(idg.at[0], idg.at[i], id_s.at[i], id_r.at[i], sibling).wait_recv()
 
     def prep_x(i):
@@ -263,7 +269,7 @@
 
     lax.fori_loop(0, SIDE, second, 0)
     for i in range(1, SIDE):
-        remote(la_ref, lag.at[0], la_s.at[i], la_r.at[i], sibling).wait_recv()
+        remote(lag.at[xme], lag.at[0], la_s.at[i], la_r.at[i], sibling).wait_recv()
 
     def potential(a):
         xi = gray((a - xme + SIDE) % SIDE)
@@ -395,7 +401,7 @@
     u, lse = pl.pallas_call(
         kernel,
         out_shape=(jax.ShapeDtypeStruct((8, 128), f32), jax.ShapeDtypeStruct((16, 128), f32)),
-        in_specs=[pl.BlockSpec(memory_space=pltpu.VMEM)] * 6,
+        in_specs=[pl.BlockSpec(memory_space=pl.ANY)] * 6,
         out_specs=(pl.BlockSpec(memory_space=pltpu.VMEM),) * 2,
         scratch_shapes=[
             pltpu.VMEM((SIDE, LAT, SBD * BC), f32),
@@ -414,7 +420,12 @@
             pltpu.VMEM((SIDE * SIDE, SBD * KC, BC), jnp.int32),
             pltpu.VMEM((SIDE + 2, 16, 128), f32),
             pltpu.VMEM((2, ROWS, 16, 128), f32),
-        ] + [dma4] * 14 + [pltpu.SemaphoreType.DMA((SIDE, SIDE))] * 2 + [pltpu.SemaphoreType.DMA((ROWS // 2,))] * 2 + [pltpu.SemaphoreType.DMA],
+        ] + [dma4] * 14 + [pltpu.SemaphoreType.DMA((SIDE, SIDE))] * 2 + [pltpu.SemaphoreType.DMA((ROWS // 2,))] * 2 + [
+            pltpu.SemaphoreType.DMA,
+            pltpu.SemaphoreType.DMA((6,)),
+            pltpu.VMEM((KC, ROWS * SBD), jnp.int32),
+            pltpu.VMEM((1, ROWS * SBD), jnp.int32),
+        ],
         compiler_params=pltpu.CompilerParams(
             collective_id=0, has_side_effects=True, vmem_limit_bytes=63 * 2**20),
         name="sinkhorn",

time: 61.8 us -> 61 us (0.987)
  Pallas kernels: 61 us -> 60.2 us
    pallas_call x1, Pallas kernels: 59.7 us -> 58.9 us  [per_device(): pl.pallas_call(kernel, out_shape=(jax.ShapeDtypeStruct((8, 128), f32), ja...]
where the time goes in v4:
time: 61 us; the launch traced here: 60.8 us
  Pallas kernels  60.2 us (99%)
  between operations  0.64 us (1%)
    pallas_call x1, Pallas kernels, per_device(): pl.pallas_call(kernel, out_shape=(jax.ShapeDtypeStruct((8, 128), f32), ja...  58.9 us
    pallas_call x1, Pallas kernels, per_device(): pl.pallas_call(finish, out_shape=(jax.ShapeDtypeStruct((8, 128), f32), ja...  1.34 us

profile of v4, /device:TPU:1, one launch (start us, length us, event | category | flops | bytes accessed | tf_op | source)
XLA Modules:
  0.0 60.8 jit_solution(5544837663455810754)
XLA Ops:
  0.6 58.9 %sinkhorn.1 = (f32[8,128]{1,0:T(8,128)}, f32[16,128]{1,0:T(8,128)}) custom-call(f32[32,1024]{1,0:T(8,128)} %x_ref.1, f32[32,2048]{1,0:T(8,128)} %y_ref.1, f32[8,128]{1,0:T(8,128)} %bitcast.12, f32[16,128]{1,0:T(8,128)} %bitcast.9, s32[4,64]{1,0:T(4,128)} %bitcast.13, s32[1,64]{1,0:T(1,128)} %bitcast.14), custom_call_target="tpu_custom_call" | custom-call | tf_op jit(solution)/shard_map/sinkhorn/pallas_call | solution.py:401
  59.5 1.3 %finish.1 = (f32[8,128]{1,0:T(8,128)}, f32[16,128]{1,0:T(8,128)}) custom-call(f32[8,128]{1,0:T(8,128)} %get-tuple-element.6.u_ref, f32[16,128]{1,0:T(8,128)} %get-tuple-element.7.lse_ref, f32[16,128]{1,0:T(8,128)} %bitcast.10, f32[16,128]{1,0:T(8,128)} %bitcast.11), custom_call_target="tpu_custom_call" | custom-call | tf_op jit(solution)/shard_map/finish/pallas_call | solution.py:434
